TPU v7x, 256 devices: a whole 4x4x8 slice. The times are simulated.
256 devices in a mesh: fsdp: 64 (over x, z, core), grp: 4 (over y).
Axes of the slice: x: 4, y: 4, z: 8, core: 2. Of those that a mesh axis runs over, the one named last changes fastest.
Arguments:
- right_factor: bfloat16 [64, 1024, 1024], P(None, 'fsdp', 'grp')
- left_factor: bfloat16 [64, 512, 512], P(None, 'fsdp', 'grp')
- right_basis: float32 [64, 1024, 1024], P(None, 'fsdp', 'grp')
- left_basis: float32 [64, 512, 512], P(None, 'fsdp', 'grp')
- moment: bfloat16 [64, 512, 1024], P(None, 'fsdp', 'grp'), may hold values from -6 to 6
- owner: int32 [64], replicated, may hold values from 0 to 63, as said below
- row_extent: int32 [64], replicated, may hold values from 256 to 512
- col_extent: int32 [64], replicated, may hold values from 512 to 1024
Outputs:
- right_refreshed: float32 [64, 2, 1024, 1024], P('fsdp', None, None, 'grp')
- left_refreshed: float32 [64, 2, 512, 512], P('fsdp', None, None, 'grp')
- new_moment: bfloat16 [64, 512, 1024], P(None, 'fsdp', 'grp')
Inputs may be any that keep to these rules, and one draw needn't show every extreme that they name: At most 2 blocks share an owner; in every draw some owner holds exactly 2 blocks and some owners hold none.
All inputs are finite; a program needn't handle non-finite values.
Results may differ from a plain program's by a relative error of at most 0.0085.
Values may be sent and summed in bfloat16 or wider, within the bound.
No kernel may reach another device: no remote copies, remote signals or barrier semaphores. Data moves between devices by JAX's collectives and lax.ppermute only.
A program may use at most 128 MiB of HBM per device.

v0:
```python
import functools

import jax
import jax.numpy as jnp
from jax import lax
from jax.experimental import pallas as pl
from jax.experimental.pallas import tpu as pltpu
from jax.sharding import PartitionSpec as P

MOST = 2
TILE = 128
SLAB = 8
HIGHEST = lax.Precision.HIGHEST
BF16 = jnp.bfloat16
F32 = jnp.float32


def lane_copy(tile, lane):
    return jnp.broadcast_to(tile[:, lane : lane + 1], (SLAB, TILE))


def row_copy(tile, row):
    return jnp.broadcast_to(tile[row : row + 1, :], (SLAB, TILE))


def tile_inverse(rows):
    lane = lax.broadcasted_iota(jnp.int32, (SLAB, TILE), 1)
    sub = lax.broadcasted_iota(jnp.int32, (SLAB, TILE), 0)
    count = len(rows)
    diagonal = [lane == sub + SLAB * s for s in range(count)]
    marked = [jnp.where(diagonal[s], rows[s], 0.0) for s in range(count)]
    while len(marked) > 1:
        marked = [marked[i] + marked[i + 1] for i in range(0, len(marked), 2)]
    across = lax.rsqrt(jnp.broadcast_to(jnp.sum(marked[0], axis=0, keepdims=True), (SLAB, TILE)))
    down = [
        jnp.broadcast_to(
            jnp.sum(jnp.where(diagonal[s], across, 0.0), axis=1, keepdims=True), (SLAB, TILE)
        )
        for s in range(count)
    ]
    rows = [rows[s] * across * down[s] for s in range(count)]
    for s in range(count):
        start = SLAB * s
        inside = (lane >= start) & (lane < start + SLAB)
        columns = [lane_copy(rows[s], start + c) for c in range(SLAB)]
        forward = jnp.where(inside, (lane - start == sub).astype(F32), rows[s])
        full = forward
        for k in range(0, SLAB, 2):
            first = columns[k]
            second = columns[k + 1]
            a = row_copy(first, k)
            b = row_copy(second, k)
            c = row_copy(second, k + 1)
            det = a * c - b * b
            pair = (sub == k) | (sub == k + 1)
            first = jnp.where(sub == k, -1.0, jnp.where(sub == k + 1, 0.0, first))
            second = jnp.where(sub == k + 1, -1.0, jnp.where(sub == k, 0.0, second))

            def parts(value):
                upper = row_copy(value, k)
                lower = row_copy(value, k + 1)
                reduced = a * lower - b * upper
                change = first * (c * upper - b * lower) + second * reduced
                return jnp.where(pair, 0.0, value), change, upper, reduced

            later = [parts(columns[q]) for q in range(k + 2, SLAB)]
            below = parts(forward)
            both = parts(full)
            inverse_det = 1.0 / det
            inverse_root = lax.rsqrt(a)
            for q, (kept, change, _, _) in enumerate(later):
                columns[k + 2 + q] = kept - change * inverse_det
            full = both[0] - both[1] * inverse_det
            forward = jnp.where(sub > k + 1, below[0] - below[1] * inverse_det, forward)
            forward = jnp.where(sub == k, below[2] * inverse_root, forward)
            forward = jnp.where(
                sub == k + 1, below[3] * (inverse_root * lax.rsqrt(det)), forward
            )
        rows[s] = forward
        if s + 1 < count:
            spread = [row_copy(full, j) for j in range(SLAB)]
        for i in range(s + 1, count):
            total = jnp.where(inside, 0.0, rows[i])
            for j in range(SLAB):
                total = total - lane_copy(rows[i], start + j) * spread[j]
            rows[i] = total
    return [jnp.where(lane <= sub + SLAB * s, rows[s] * across, 0.0) for s in range(count)]


def dot32(a, b, dims=((1,), (0,))):
    return lax.dot_general(a, b, (dims, ((), ())), precision=HIGHEST, preferred_element_type=F32)


def dot(a, b, dims=((1,), (0,))):
    return lax.dot_general(a, b, (dims, ((), ())), preferred_element_type=F32)


def read_slabs(tile_ref):
    return [tile_ref[SLAB * i : SLAB * (i + 1), :] for i in range(TILE // SLAB)]


def write_slabs(tile_ref, slabs):
    for i, slab in enumerate(slabs):
        tile_ref[SLAB * i : SLAB * (i + 1), :] = slab


def split3(value):
    high = value.astype(BF16)
    rest = value - high.astype(F32)
    middle = rest.astype(BF16)
    return high, middle, (rest - middle.astype(F32)).astype(BF16)


def left6(value):
    high, middle, small = split3(value)
    return jnp.concatenate([high, high, middle, middle, high, small], axis=1)


def right6(value, axis=0):
    high, middle, small = split3(value)
    return jnp.concatenate([high, middle, high, middle, small, high], axis=axis)


def invert(mat, tile, row, low):
    order = mat.shape[0]
    chunk = 256
    tile[...] = mat[:TILE, :TILE]
    write_slabs(tile, tile_inverse(read_slabs(tile)))
    lanes = lax.broadcasted_iota(jnp.int32, (TILE, order), 1)

    row_ids = lax.broadcasted_iota(jnp.int32, (order, TILE), 0)

    def step(k, carry):
        start = pl.multiple_of(k * TILE, TILE)
        after = pl.multiple_of(start + TILE, TILE)
        own = pl.ds(start, TILE)
        following = pl.ds(after, TILE)
        inverse = tile[...]
        near_upper = dot32(inverse, mat[own, following])
        near_side = dot32(mat[following, own], inverse, ((1,), (1,)))
        tile[...] = mat[following, following] - dot32(near_side, near_upper)
        row[...] = dot(left6(inverse), right6(mat[own, :]))
        row[:, own] = inverse
        column = mat[:, own]
        low[...] = jnp.where(row_ids >= after, dot(left6(column), right6(inverse, 1), ((1,), (1,))), 0.0)
        mat[:, own] = jnp.where(row_ids >= after, 0.0, column)
        mat[own, :] = jnp.where(lanes < after, row[...], 0.0)
        slabs = read_slabs(tile)
        lower = left6(low[...])
        upper = right6(row[...])
        for c in range(0, order, chunk):
            mat[:, c : c + chunk] -= dot(lower, upper[:, c : c + chunk])
        write_slabs(tile, tile_inverse(slabs))
        return carry

    lax.fori_loop(0, order // TILE - 1, step, 0)
    last = order - TILE
    inverse = tile[...]
    mat[last:, :] = dot32(inverse, mat[last:, :])
    mat[last:, last:] = inverse


def split32(value):
    high = value.astype(BF16)
    return high, (value - high.astype(F32)).astype(BF16)


def collect(group, pieces, targets):
    own, following, previous, far_top, far_bottom = pieces
    half, width = far_top.shape
    halves = [[piece.at[pl.ds(half * t, half), :] for t in range(2)] for piece in (own, following, previous)]
    for shift, pair in zip((0, 1, 3, 2), halves + [[far_top, far_bottom]]):
        columns = pl.ds(pl.multiple_of(lax.rem(group + shift, 4) * width, TILE), width)
        for source, target in zip(pair, targets):
            target[:, columns] = source[...]


def power_gram(group, pieces, factor, basis, power, mat):
    order, width = pieces[3].shape
    collect(group, pieces, (factor, basis))
    for c in range(0, order, width):
        power[:, c : c + width] = dot(factor[...], basis[:, c : c + width]).astype(BF16)
    for c in range(0, order, width):
        mat[:, c : c + width] = dot(power[...], power[:, c : c + width], ((0,), (0,)))


def fresh_of(power, inverse_rows):
    across = ((1,), (1,))
    high, low_part = split32(inverse_rows)
    total = dot(power[...], high, across) + dot(power[...], low_part, across)
    return total.astype(BF16)


def left_kernel(first, *refs):
    pieces, (fresh, mixer, factor, basis, power, mat), work = refs[:5], refs[5:11], refs[11:]
    power_gram(first[0], pieces, factor, basis, power, mat)
    invert(mat, *work)
    fresh[...] = fresh_of(power, mat[...])
    mixer[...] = dot(fresh[...], basis[...], ((0,), (0,))).astype(BF16)


def right_kernel(first, *refs):
    pieces, moment_pieces, mixer = refs[:5], refs[5:10], refs[10]
    (fresh, out, factor, basis, power, mat, moment), work = refs[11:18], refs[18:]
    group = first[0]
    half = moment.shape[0] // 2
    width = fresh.shape[1]
    power_gram(group, pieces, factor, basis, power, mat)
    collect(group, moment_pieces, [moment.at[pl.ds(half * t, half), :] for t in range(2)])
    carried = dot(moment[...], basis[...], ((1,), (1,))).astype(BF16)
    moment[...] = carried
    invert(mat, *work)
    fresh[...] = fresh_of(power, mat[pl.ds(pl.multiple_of(group * width, TILE), width), :])
    turned = dot(moment[...], fresh[...]).astype(BF16)
    out[...] = dot(mixer[...], turned).astype(BF16)


VMEM = pl.BlockSpec(memory_space=pltpu.VMEM)
SMEM = pl.BlockSpec(memory_space=pltpu.SMEM)


def basis_call(kernel, group_index, inputs, order, out_shapes, extra, name):
    square = pltpu.VMEM((order, order), BF16)
    return pl.pallas_call(
        kernel,
        out_shape=tuple(jax.ShapeDtypeStruct(shape, BF16) for shape in out_shapes),
        in_specs=[SMEM] + [VMEM] * len(inputs),
        out_specs=(VMEM,) * len(out_shapes),
        scratch_shapes=[square, square, square, pltpu.VMEM((order, order), F32)]
        + extra
        + [
            pltpu.VMEM((TILE, TILE), F32),
            pltpu.VMEM((TILE, order), F32),
            pltpu.VMEM((order, TILE), F32),
        ],
        compiler_params=pltpu.CompilerParams(vmem_limit_bytes=40 * 2**20),
        cost_estimate=pl.CostEstimate(
            flops=5 * 10**7 * order, bytes_accessed=10 * order**2, transcendentals=0
        ),
        name=name,
    )(group_index, *inputs)


def left_call(group_index, pieces):
    order = pieces[3].shape[0]
    shapes = [(order, order)] * 2
    return basis_call(left_kernel, group_index, pieces, order, shapes, [], "left_basis")


def right_call(group_index, pieces, moment_pieces, mixer):
    order, width = pieces[3].shape
    rows = mixer.shape[0]
    return basis_call(
        right_kernel,
        group_index,
        (*pieces, *moment_pieces, mixer),
        order,
        [(order, width), (rows, width)],
        [pltpu.VMEM((rows, order), BF16)],
        "right_basis",
    )


def pack_kernel(places, blocks, row_extent, col_extent, factor_r, factor_l, basis_r, basis_l, moment, out):
    rows_r, cols_r = factor_r.shape[1:]
    rows_l, cols_l = factor_l.shape[1:]

    def ids(rows, cols):
        return (
            lax.broadcasted_iota(jnp.int32, (rows, cols), 0) + places[0] * rows,
            lax.broadcasted_iota(jnp.int32, (rows, cols), 1) + places[1] * cols,
        )

    row_r, col_r = ids(rows_r, cols_r)
    row_l, col_l = ids(rows_l, cols_l)
    unit_r = (row_r == col_r).astype(F32)
    unit_l = (row_l == col_l).astype(F32)
    most_r = jnp.maximum(row_r, col_r)
    most_l = jnp.maximum(row_l, col_l)

    def step(r, carry):
        b = jnp.clip(blocks[r], 0, factor_r.shape[0] - 1)
        masked = jnp.where(most_r < col_extent[b], factor_r[b].astype(F32), unit_r)
        out[r, :rows_r, :] = masked.astype(BF16)
        out[r, rows_r : 2 * rows_r, :] = basis_r[b].astype(BF16)
        masked = jnp.where(most_l < row_extent[b], factor_l[b].astype(F32), unit_l)
        left = jnp.concatenate([masked, basis_l[b]], axis=1)
        both = jnp.concatenate([left, moment[b].astype(F32)], axis=0)
        out[r, 2 * rows_r :, :] = both.astype(BF16)
        return carry

    lax.fori_loop(0, out.shape[0], step, 0)


def packed(places, blocks, row_extent, col_extent, *arrays):
    rows_r, cols_r = arrays[0].shape[1:]
    rows_l = arrays[1].shape[1]
    return pl.pallas_call(
        pack_kernel,
        out_shape=jax.ShapeDtypeStruct(
            (blocks.shape[0], 2 * rows_r + 2 * rows_l, cols_r), BF16
        ),
        in_specs=[SMEM] * 4 + [VMEM] * 5,
        out_specs=VMEM,
        compiler_params=pltpu.CompilerParams(vmem_limit_bytes=24 * 2**20),
        cost_estimate=pl.CostEstimate(flops=10**9, bytes_accessed=4 * 2**20, transcendentals=0),
        name="packed",
    )(places, blocks, row_extent, col_extent, *arrays)


def shifted(piece, shift):
    count = lax.axis_size("grp")
    return lax.ppermute(piece, "grp", [(i, (i + shift) % count) for i in range(count)])


def near(piece):
    return shifted(piece, 1), shifted(piece, -1)


def gathered(piece, previous, following):
    half = piece.shape[0] // 2
    return piece, following, previous, shifted(previous[:half], 1), shifted(following[half:], -1)


def gathered_at_once(piece):
    half = piece.shape[0] // 2
    return (
        piece,
        shifted(piece, -1),
        shifted(piece, 1),
        shifted(piece[:half], 2),
        shifted(piece[half:], -2),
    )


def eye_piece(row_count, col_count, col_start):
    row_ids = lax.broadcasted_iota(jnp.int32, (row_count, col_count), 0)
    col_ids = lax.broadcasted_iota(jnp.int32, (row_count, col_count), 1) + col_start
    return (row_ids == col_ids).astype(F32)


def placement(owner, owner_count):
    block_ids = jnp.arange(owner.shape[0], dtype=jnp.int32)
    rows = jnp.arange(owner_count, dtype=jnp.int32)

    def total(hits, values):
        return jnp.sum(jnp.where(hits, values, 0), axis=1)

    earlier = (owner[:, None] == owner[None, :]) & (block_ids[None, :] < block_ids[:, None])
    repeated = jnp.any(earlier, axis=1)
    owned = rows[:, None] == owner[None, :]
    first_hits = owned & ~repeated[None, :]
    second_hits = owned & repeated[None, :]
    has_first = jnp.any(first_hits, axis=1)
    has_second = jnp.any(second_hits, axis=1)
    before = rows[None, :] < rows[:, None]
    empty_rank = total(before & ~has_first[None, :], 1)
    double_rank = total(before & has_second[None, :], 1)
    matched = ~has_first[:, None] & has_second[None, :] & (empty_rank[:, None] == double_rank[None, :])
    second_of = total(second_hits, block_ids[None, :])
    row_block = total(first_hits, block_ids[None, :]) + total(matched, second_of[None, :])
    second_row = jnp.sum(jnp.where(matched, rows[:, None], 0), axis=0)
    row_of = total(block_ids[:, None] == row_block[None, :], rows[None, :])
    return (row_block, row_of, second_row, has_first, has_second)


def pick(values, indices):
    return jnp.take(values, indices, axis=0, mode="clip")


def swap(pieces):
    return lax.all_to_all(pieces, "fsdp", split_axis=0, concat_axis=0, tiled=True)


def per_device(
    right_factor, left_factor, right_basis, left_basis, moment, owner, row_extent, col_extent
):
    owner_count = lax.axis_size("fsdp")
    fsdp_index = lax.axis_index("fsdp")
    group_index = lax.axis_index("grp")
    right_rows, right_cols = right_factor.shape[1:]
    left_rows, left_cols = left_factor.shape[1:]
    order_r = right_rows * owner_count
    order_l = left_rows * owner_count
    row_block, row_of, second_row, has_first, has_second = placement(owner, owner_count)
    group = group_index.astype(jnp.int32)[None]
    places = jnp.stack([fsdp_index, group_index]).astype(jnp.int32)
    pack = packed(
        places,
        row_block,
        row_extent,
        col_extent,
        right_factor,
        left_factor,
        right_basis,
        left_basis,
        moment,
    )
    pack = swap(pack)
    bounds = (0, right_rows, 2 * right_rows, 2 * right_rows + left_rows, 2 * (right_rows + left_rows))
    factor_r, basis_r, left_pair, moment_in = (
        pack[:, start:stop].reshape(-1, right_cols) for start, stop in zip(bounds, bounds[1:])
    )
    left_piece = jnp.concatenate([left_pair[:, :left_cols], left_pair[:, left_cols:]], axis=0)
    right_piece = jnp.concatenate([factor_r, basis_r], axis=0)

    left_pieces = gathered(left_piece, *near(left_piece))
    left_pieces, right_piece = lax.optimization_barrier((left_pieces, right_piece))
    right_near = near(right_piece)
    fresh_l, mixer = left_call(group, left_pieces)
    fresh_l, right_near = lax.optimization_barrier((fresh_l, right_near))
    left_new = lax.dynamic_slice_in_dim(fresh_l, group_index * left_cols, left_cols, 1)
    rows_l = swap(left_new.reshape(owner_count, left_rows, left_cols))
    right_near, moment_in = lax.optimization_barrier((right_near, moment_in))
    right_pieces = gathered(right_piece, *right_near)
    moment_pieces = gathered_at_once(moment_in)
    fresh_r, moment_out = right_call(group, right_pieces, moment_pieces, mixer)
    fresh_r, rows_l = lax.optimization_barrier((fresh_r, rows_l))

    by_row = fresh_r.reshape(owner_count, MOST, left_rows, right_cols)
    back = jnp.concatenate(
        [
            by_row[:, 0],
            by_row[:, 1],
            moment_out.reshape(owner_count, left_rows, right_cols),
            pick(rows_l, second_row),
        ],
        axis=2,
    )
    back = swap(back)
    wide = MOST * right_cols
    second_r = swap(pick(back[:, :, :wide], second_row))
    second_r = jnp.stack([second_r[:, :, :right_cols], second_r[:, :, right_cols:]], axis=1)
    second_r = second_r.reshape(order_r, right_cols)
    second_l = back[:, :, wide + right_cols :].reshape(order_l, left_cols)
    new_moment = pick(back[:, :, wide : wide + right_cols], row_of)

    def slots(own, second):
        order, width = own.shape
        unit = eye_piece(order, width, group_index * width)
        filled = (
            lax.dynamic_index_in_dim(has, fsdp_index, keepdims=False)
            for has in (has_first, has_second)
        )
        pair = [jnp.where(has, new.astype(F32), unit) for has, new in zip(filled, (own, second))]
        return jnp.stack(pair)[None]

    return (slots(fresh_r, second_r), slots(left_new, second_l), new_moment)


def solution(mesh):
    return jax.shard_map(
        per_device,
        mesh=mesh,
        in_specs=(
            P(None, "fsdp", "grp"),
            P(None, "fsdp", "grp"),
            P(None, "fsdp", "grp"),
            P(None, "fsdp", "grp"),
            P(None, "fsdp", "grp"),
            P(),
            P(),
            P(),
        ),
        out_specs=(
            P("fsdp", None, None, "grp"),
            P("fsdp", None, None, "grp"),
            P(None, "fsdp", "grp"),
        ),
        check_vma=False,
    )
```

profile of v0, /device:TPU:1, one launch (start us, length us, event | category | flops | bytes accessed | tf_op | source)
XLA Modules:
  0.0 251.5 jit_solution(14932952498608833762)
XLA Ops:
  0.6 0.9 fusion.7
  1.6 0.8 fusion.5
  2.4 0.1 select_reduce_fusion.5
  2.5 0.8 select_reduce_fusion.3
  3.3 0.1 pad_add_fusion.places
  3.4 0.2 select_reduce_fusion.1
  3.6 0.0 copy-start
  3.6 1.2 copy-done
  4.8 1.0 copy-done.1
  5.8 0.9 copy-done.2
  6.8 0.9 copy-done.3
  7.7 0.9 copy-done.6
  8.7 0.7 copy-done.8
  9.3 0.7 copy-done.9
  10.0 1.4 packed.1
  11.4 52.6 %all_to_all.20 = bf16[64,48,256]{2,1,0:T(8,128)(2,1)S(1)} all-to-all(bf16[64,48,256]{2,1,0:T(8,128)(2,1)S(1)} %packed.1), channel_id=1, replica_groups=mesh['fsdp'=64,'grp'=4] {'fsdp'}, dimensions={0} | all-to-all | bytes 3145728 | tf_op jit(solution)/shard_map/all_to_all | solution.py:372
  64.1 1.4 collective-permute-start.1
  65.4 1.5 collective-permute-start
  67.0 0.1 fusion.8
  67.0 6.2 %collective-permute-done.1.refs_2_ = bf16[1024,128]{1,0:T(8,128)(2,1)S(1)} collective-permute-done((bf16[1024,128]{1,0:T(8,128)(2,1)S(1)}, bf16[1024,128]{1,0:T(8,128)(2,1)S(1)}, u32[]{:S(2)}, u32[]{:S(2)}) %collective-permute-start.1) | collective-permute-done | bytes 262176 | tf_op jit(solution)/shard_map/ppermute | solution.py:313
  73.3 0.1 collective-permute-start.2
  73.4 2.7 %collective-permute-start.3 = (bf16[512,128]{1,0:T(8,128)(2,1)S(1)}, bf16[512,128]{1,0:T(8,128)(2,1)S(1)}, u32[]{:S(2)}, u32[]{:S(2)}) collective-permute-start(bf16[512,128]{1,0:T(8,128)(2,1)S(1)} %slice.86), channel_id=1, source_target_pairs={{0,3},{1,0},{2,1},{3,2},{4,7},{5,4},{6,5},{7,6},{8,11},{9,8},{10,9... | collective-permute-start | bytes 393224 | tf_op jit(solution)/shard_map/ppermute | solution.py:313
  76.1 0.1 pad_maximum_fusion.refs_0_
  76.2 2.5 collective-permute-done.2.refs_3_
  78.7 2.5 collective-permute-start.5
  81.1 19.3 %left_basis.1 = (bf16[512,512]{1,0:T(8,128)(2,1)S(1)}, bf16[512,512]{1,0:T(8,128)(2,1)S(1)}) custom-call(s32[1]{0:T(128)} %bitcast.1.first, bf16[1024,128]{1,0:T(8,128)(2,1)S(1)} %pad_maximum_fusion.2.refs_0_, bf16[1024,128]{1,0:T(8,128)(2,1)S(1)} %collective-permute-done.refs_1_, bf16[1024,128]{1,0:T(8,128)(2,1)S(1)} %collective-permute-done.1.refs_2_, ...), custom_call_target="tpu_custom_call" | custom-call | flops 25600000000 | bytes 2621440 | tf_op jit(solution)/shard_map/left_basis/pallas_call | solution.py:224
  100.4 1.1 collective-permute-done.5.refs_1_
  101.5 2.9 %collective-permute-done.4.refs_2_ = bf16[2048,256]{1,0:T(8,128)(2,1)S(1)} collective-permute-done((bf16[2048,256]{1,0:T(8,128)(2,1)S(1)}, bf16[2048,256]{1,0:T(8,128)(2,1)S(1)}, u32[]{:S(2)}, u32[]{:S(2)}) %collective-permute-start.4) | collective-permute-done | bytes 1048608 | tf_op jit(solution)/shard_map/ppermute | solution.py:313
  104.4 0.9 slice.66
  105.3 0.8 slice.65
  106.1 2.7 %collective-permute-start.7 = (bf16[1024,256]{1,0:T(8,128)(2,1)}, bf16[1024,256]{1,0:T(8,128)(2,1)}, u32[]{:S(2)}, u32[]{:S(2)}) collective-permute-start(bf16[1024,256]{1,0:T(8,128)(2,1)} %slice.66), channel_id=1, source_target_pairs={{0,3},{1,0},{2,1},{3,2},{4,7},{5,4},{6,5},{7,6},{8,11},{9,8},{10,9... | collective-permute-start | bytes 1572872 | tf_op jit(solution)/shard_map/ppermute | solution.py:313
  108.8 0.7 fusion.9
  109.5 0.6 collective-permute-start.9
  110.1 2.1 collective-permute-start.8
  112.2 6.9 %collective-permute-done.11.refs_9_ = bf16[256,256]{1,0:T(8,128)(2,1)S(1)} collective-permute-done((bf16[256,256]{1,0:T(8,128)(2,1)S(1)}, bf16[256,256]{1,0:T(8,128)(2,1)S(1)}, u32[]{:S(2)}, u32[]{:S(2)}) %collective-permute-start.11) | collective-permute-done | bytes 131104 | tf_op jit(solution)/shard_map/ppermute | solution.py:313
  119.0 1.5 collective-permute-start.10
  120.5 0.7 dynamic-slice_bitcast_fusion
  121.2 15.6 %all-to-all-start.1 = ((bf16[64,8,128]{2,1,0:T(8,128)(2,1)}), bf16[64,8,128]{2,1,0:T(8,128)(2,1)}, u32[]{:S(2)}, u32[]{:S(2)}) async-start(bf16[64,8,128]{2,1,0:T(8,128)(2,1)} %dynamic-slice_bitcast_fusion), calls=%async_computation.1 | async-start | bytes 262144 | tf_op jit(solution)/shard_map/all_to_all | solution.py:372
  136.9 0.0 copy-start.10
  136.9 0.7 copy-done.10
  137.6 0.0 copy-start.5
  137.6 1.2 copy-done.5
  138.8 0.9 copy-done.11
  139.8 1.0 copy-done.13
  140.8 44.5 %right_basis.1 = (bf16[1024,256]{1,0:T(8,128)(2,1)S(1)}, bf16[512,256]{1,0:T(8,128)(2,1)S(1)}) custom-call(s32[1]{0:T(128)} %bitcast.1.first, bf16[2048,256]{1,0:T(8,128)(2,1)S(1)} %pad_maximum_fusion.refs_0_, bf16[2048,256]{1,0:T(8,128)(2,1)S(1)} %collective-permute-done.5.refs_1_, bf16[2048,256]{1,0:T(8,128)(2,1)S(1)} %copy-done.5, ...), custom_call_target="tpu_custom_call" | custom-call | flops 51200000000 | bytes 10485760 | tf_op jit(solution)/shard_map/right_basis/pallas_call | solution.py:224
  185.3 1.5 gather_fusion
  186.9 1.0 pad_maximum_fusion.1
  187.9 10.3 %all-to-all-start.2 = ((bf16[64,8,896]{2,1,0:T(8,128)(2,1)}), bf16[64,8,896]{2,1,0:T(8,128)(2,1)S(1)}, u32[]{:S(2)}, u32[]{:S(2)}) async-start(bf16[64,8,896]{2,1,0:T(8,128)(2,1)} %pad_maximum_fusion.1), calls=%async_computation.2 | async-start | bytes 1835008 | tf_op jit(solution)/shard_map/all_to_all | solution.py:372
  198.2 0.7 dynamic_slice.14
  198.9 0.6 dynamic_slice.12
  199.4 0.1 select_reduce_fusion
  199.5 24.4 %all-to-all-done.2 = bf16[64,8,896]{2,1,0:T(8,128)(2,1)S(1)} async-done(((bf16[64,8,896]{2,1,0:T(8,128)(2,1)}), bf16[64,8,896]{2,1,0:T(8,128)(2,1)S(1)}, u32[]{:S(2)}, u32[]{:S(2)}) %all-to-all-start.2) | async-done | bytes 917536 | tf_op jit(solution)/shard_map/all_to_all | solution.py:372
  224.0 1.4 gather_fusion.1
  225.4 6.2 %all-to-all-start.3 = ((bf16[64,8,512]{2,1,0:T(8,128)(2,1)}), bf16[64,8,512]{2,1,0:T(8,128)(2,1)S(1)}, u32[]{:S(2)}, u32[]{:S(2)}) async-start(bf16[64,8,512]{2,1,0:T(8,128)(2,1)} %gather_fusion.1), calls=%async_computation.3 | async-start | bytes 1048576 | tf_op jit(solution)/shard_map/all_to_all | solution.py:372
  231.6 1.6 select_bitcast_fusion.1
  233.2 0.8 select_bitcast_fusion
  234.1 1.3 gather_fusion.2
  235.4 0.7 convert_select_fusion.1
  236.1 0.8 maximum_bitcast_fusion.1
  236.9 12.0 %all-to-all-done.3 = bf16[64,8,512]{2,1,0:T(8,128)(2,1)S(1)} async-done(((bf16[64,8,512]{2,1,0:T(8,128)(2,1)}), bf16[64,8,512]{2,1,0:T(8,128)(2,1)S(1)}, u32[]{:S(2)}, u32[]{:S(2)}) %all-to-all-start.3) | async-done | bytes 524320 | tf_op jit(solution)/shard_map/all_to_all | solution.py:372
  249.0 0.1 maximum_convert_fusion
  249.0 0.1 copy.19
  249.2 0.8 convert_select_fusion
  250.0 1.5 maximum_bitcast_fusion
  (41 shorter events, 0.3 us)
Async XLA Ops:
  3.6 1.2 copy-start
  4.8 1.0 copy-start.1
  5.8 0.9 copy-start.2
  6.8 0.9 copy-start.3
  7.7 0.9 copy-start.6
  8.7 0.7 copy-start.8
  9.3 0.7 copy-start.9
  64.1 9.2 %collective-permute-start.1 = (bf16[1024,128]{1,0:T(8,128)(2,1)S(1)}, bf16[1024,128]{1,0:T(8,128)(2,1)S(1)}, u32[]{:S(2)}, u32[]{:S(2)}) collective-permute-start(bf16[1024,128]{1,0:T(8,128)(2,1)S(1)} %pad_maximum_fusion.2.refs_0_), channel_id=1, source_target_pairs={{0,1},{1,2},{2,3},{3,0},{4,5},{5,6},{6,7},{7,4},{8,9},{9,10},{10,1... | collective-permute-start | bytes 786440 | tf_op jit(solution)/shard_map/ppermute | solution.py:313
  65.4 7.9 %collective-permute-start = (bf16[1024,128]{1,0:T(8,128)(2,1)S(1)}, bf16[1024,128]{1,0:T(8,128)(2,1)S(1)}, u32[]{:S(2)}, u32[]{:S(2)}) collective-permute-start(bf16[1024,128]{1,0:T(8,128)(2,1)S(1)} %pad_maximum_fusion.2.refs_0_), channel_id=1, source_target_pairs={{0,3},{1,0},{2,1},{3,2},{4,7},{5,4},{6,5},{7,6},{8,11},{9,8},{10,9... | collective-permute-start | bytes 786440 | tf_op jit(solution)/shard_map/ppermute | solution.py:313
  73.3 5.4 %collective-permute-start.2 = (bf16[512,128]{1,0:T(8,128)(2,1)S(1)}, bf16[512,128]{1,0:T(8,128)(2,1)S(1)}, u32[]{:S(2)}, u32[]{:S(2)}) collective-permute-start(bf16[512,128]{1,0:T(8,128)(2,1)S(1)} %slice.85), channel_id=1, source_target_pairs={{0,1},{1,2},{2,3},{3,0},{4,5},{5,6},{6,7},{7,4},{8,9},{9,10},{10,1... | collective-permute-start | bytes 393224 | tf_op jit(solution)/shard_map/ppermute | solution.py:313
  73.4 5.3 %collective-permute-start.3 = (bf16[512,128]{1,0:T(8,128)(2,1)S(1)}, bf16[512,128]{1,0:T(8,128)(2,1)S(1)}, u32[]{:S(2)}, u32[]{:S(2)}) collective-permute-start(bf16[512,128]{1,0:T(8,128)(2,1)S(1)} %slice.86), channel_id=1, source_target_pairs={{0,3},{1,0},{2,1},{3,2},{4,7},{5,4},{6,5},{7,6},{8,11},{9,8},{10,9... | collective-permute-start | bytes 393224 | tf_op jit(solution)/shard_map/ppermute | solution.py:313
  78.7 22.9 %collective-permute-start.5 = (bf16[2048,256]{1,0:T(8,128)(2,1)S(1)}, bf16[2048,256]{1,0:T(8,128)(2,1)S(1)}, u32[]{:S(2)}, u32[]{:S(2)}) collective-permute-start(bf16[2048,256]{1,0:T(8,128)(2,1)S(1)} %pad_maximum_fusion.refs_0_), channel_id=1, source_target_pairs={{0,3},{1,0},{2,1},{3,2},{4,7},{5,4},{6,5},{7,6},{8,11},{9,8},{10,9... | collective-permute-start | bytes 3145736 | tf_op jit(solution)/shard_map/ppermute | solution.py:313
  81.1 23.3 %collective-permute-start.4 = (bf16[2048,256]{1,0:T(8,128)(2,1)S(1)}, bf16[2048,256]{1,0:T(8,128)(2,1)S(1)}, u32[]{:S(2)}, u32[]{:S(2)}) collective-permute-start(bf16[2048,256]{1,0:T(8,128)(2,1)S(1)} %pad_maximum_fusion.refs_0_), channel_id=1, source_target_pairs={{0,1},{1,2},{2,3},{3,0},{4,5},{5,6},{6,7},{7,4},{8,9},{9,10},{10,1... | collective-permute-start | bytes 3145736 | tf_op jit(solution)/shard_map/ppermute | solution.py:313
  100.4 18.6 %copy-start.12 = (bf16[512,512]{1,0:T(8,128)(2,1)}, bf16[512,512]{1,0:T(8,128)(2,1)S(1)}, u32[]{:S(2)}) copy-start(bf16[512,512]{1,0:T(8,128)(2,1)S(1)} %get-tuple-element.33.refs_10_) | copy-start | bytes 1572868
  100.4 37.1 %copy-start.7 = (bf16[512,512]{1,0:T(8,128)(2,1)}, bf16[512,512]{1,0:T(8,128)(2,1)S(1)}, u32[]{:S(2)}) copy-start(bf16[512,512]{1,0:T(8,128)(2,1)S(1)} %get-tuple-element.35) | copy-start | bytes 1572868
  104.4 5.1 %copy-start.4 = (bf16[2048,256]{1,0:T(8,128)(2,1)}, bf16[2048,256]{1,0:T(8,128)(2,1)S(1)}, u32[]{:S(2)}) copy-start(bf16[2048,256]{1,0:T(8,128)(2,1)S(1)} %collective-permute-done.4.refs_2_) | copy-start | bytes 3145732
  106.1 31.4 %collective-permute-start.6 = (bf16[1024,256]{1,0:T(8,128)(2,1)}, bf16[1024,256]{1,0:T(8,128)(2,1)}, u32[]{:S(2)}, u32[]{:S(2)}) collective-permute-start(bf16[1024,256]{1,0:T(8,128)(2,1)} %slice.65), channel_id=1, source_target_pairs={{0,1},{1,2},{2,3},{3,0},{4,5},{5,6},{6,7},{7,4},{8,9},{9,10},{10,1... | collective-permute-start | bytes 1572872 | tf_op jit(solution)/shard_map/ppermute | solution.py:313
  106.1 31.4 %collective-permute-start.7 = (bf16[1024,256]{1,0:T(8,128)(2,1)}, bf16[1024,256]{1,0:T(8,128)(2,1)}, u32[]{:S(2)}, u32[]{:S(2)}) collective-permute-start(bf16[1024,256]{1,0:T(8,128)(2,1)} %slice.66), channel_id=1, source_target_pairs={{0,3},{1,0},{2,1},{3,2},{4,7},{5,4},{6,5},{7,6},{8,11},{9,8},{10,9... | collective-permute-start | bytes 1572872 | tf_op jit(solution)/shard_map/ppermute | solution.py:313
  109.5 9.6 %collective-permute-start.11 = (bf16[256,256]{1,0:T(8,128)(2,1)S(1)}, bf16[256,256]{1,0:T(8,128)(2,1)S(1)}, u32[]{:S(2)}, u32[]{:S(2)}) collective-permute-start(bf16[256,256]{1,0:T(8,128)(2,1)S(1)} %get-tuple-element.53), channel_id=1, source_target_pairs={{0,2},{1,3},{2,0},{3,1},{4,6},{5,7},{6,4},{7,5},{8,10},{9,11},{10,... | collective-permute-start | bytes 393224 | tf_op jit(solution)/shard_map/ppermute | solution.py:313
  109.5 27.4 %collective-permute-start.9 = (bf16[512,256]{1,0:T(8,128)(2,1)S(1)}, bf16[512,256]{1,0:T(8,128)(2,1)S(1)}, u32[]{:S(2)}, u32[]{:S(2)}) collective-permute-start(bf16[512,256]{1,0:T(8,128)(2,1)S(1)} %get-tuple-element.32.refs_5_), channel_id=1, source_target_pairs={{0,1},{1,2},{2,3},{3,0},{4,5},{5,6},{6,7},{7,4},{8,9},{9,10},{10,1... | collective-permute-start | bytes 786440 | tf_op jit(solution)/shard_map/ppermute | solution.py:313
  110.1 26.8 %collective-permute-start.8 = (bf16[512,256]{1,0:T(8,128)(2,1)S(1)}, bf16[512,256]{1,0:T(8,128)(2,1)S(1)}, u32[]{:S(2)}, u32[]{:S(2)}) collective-permute-start(bf16[512,256]{1,0:T(8,128)(2,1)S(1)} %get-tuple-element.32.refs_5_), channel_id=1, source_target_pairs={{0,3},{1,0},{2,1},{3,2},{4,7},{5,4},{6,5},{7,6},{8,11},{9,8},{10,9... | collective-permute-start | bytes 786440 | tf_op jit(solution)/shard_map/ppermute | solution.py:313
  119.0 17.8 %collective-permute-start.10 = (bf16[256,256]{1,0:T(8,128)(2,1)}, bf16[256,256]{1,0:T(8,128)(2,1)}, u32[]{:S(2)}, u32[]{:S(2)}) collective-permute-start(bf16[256,256]{1,0:T(8,128)(2,1)} %get-tuple-element.54), channel_id=1, source_target_pairs={{0,2},{1,3},{2,0},{3,1},{4,6},{5,7},{6,4},{7,5},{8,10},{9,11},{10,... | collective-permute-start | bytes 393224 | tf_op jit(solution)/shard_map/ppermute | solution.py:313
  121.2 64.1 %all-to-all-start.1 = ((bf16[64,8,128]{2,1,0:T(8,128)(2,1)}), bf16[64,8,128]{2,1,0:T(8,128)(2,1)}, u32[]{:S(2)}, u32[]{:S(2)}) async-start(bf16[64,8,128]{2,1,0:T(8,128)(2,1)} %dynamic-slice_bitcast_fusion), calls=%async_computation.1 | async-start | bytes 262144 | tf_op jit(solution)/shard_map/all_to_all | solution.py:372
  136.9 0.7 copy-start.10
  137.6 1.2 copy-start.5
  138.8 0.9 copy-start.11
  139.8 1.0 copy-start.13
  187.9 36.1 %all-to-all-start.2 = ((bf16[64,8,896]{2,1,0:T(8,128)(2,1)}), bf16[64,8,896]{2,1,0:T(8,128)(2,1)S(1)}, u32[]{:S(2)}, u32[]{:S(2)}) async-start(bf16[64,8,896]{2,1,0:T(8,128)(2,1)} %pad_maximum_fusion.1), calls=%async_computation.2 | async-start | bytes 1835008 | tf_op jit(solution)/shard_map/all_to_all | solution.py:372
  225.4 23.5 %all-to-all-start.3 = ((bf16[64,8,512]{2,1,0:T(8,128)(2,1)}), bf16[64,8,512]{2,1,0:T(8,128)(2,1)S(1)}, u32[]{:S(2)}, u32[]{:S(2)}) async-start(bf16[64,8,512]{2,1,0:T(8,128)(2,1)} %gather_fusion.1), calls=%async_computation.3 | async-start | bytes 1048576 | tf_op jit(solution)/shard_map/all_to_all | solution.py:372
where the time goes:
time: 252 us; the launch traced here: 251 us
  Pallas kernels  65.2 us (26%)
  waiting for transfers between devices  56 us (22%)
  blocking collectives  52.6 us (21%)
  starting transfers between devices  47.2 us (19%)
  local copies, waits for them, and re-layouts  19.2 us (8%)
  other arithmetic  10.4 us (4%)
    pallas_call x2, Pallas kernels, basis_call(): pl.pallas_call(kernel, out_shape=tuple((jax.ShapeDtypeStruct(shape, BF16)...  63.7 us
    all_to_all x1, blocking collectives, swap(): lax.all_to_all(pieces, 'fsdp', split_axis=0, concat_axis=0, tiled=True)  52.6 us
    all_to_all x3, waiting for transfers between devices, swap(): lax.all_to_all(pieces, 'fsdp', split_axis=0, concat_axis=0, tiled=True)  36.4 us
    all_to_all x3, starting transfers between devices, swap(): lax.all_to_all(pieces, 'fsdp', split_axis=0, concat_axis=0, tiled=True)  32.1 us
    ppermute x12, waiting for transfers between devices, shifted(): lax.ppermute(piece, 'grp', [(i, (i + shift) % count) for i in range(count)])  19.6 us
    ppermute x12, starting transfers between devices, shifted(): lax.ppermute(piece, 'grp', [(i, (i + shift) % count) for i in range(count)])  15 us
    unnamed x28, local copies, waits for them, and re-layouts  10.3 us
  transfers between devices with their start and end apart: 15, of which 7 were waited for; matrix products, arithmetic and copies ran while one was open for 3% of the time, Pallas kernels for 25%

commit v1 on v0

--- a/solution.py
+++ b/solution.py
@@ -165,19 +165,22 @@
     return high, (value - high.astype(F32)).astype(BF16)
 
 
-def collect(group, pieces, targets):
+def collect(group, pieces, tops, bottoms):
     own, following, previous, far_top, far_bottom = pieces
     half, width = far_top.shape
-    halves = [[piece.at[pl.ds(half * t, half), :] for t in range(2)] for piece in (own, following, previous)]
-    for shift, pair in zip((0, 1, 3, 2), halves + [[far_top, far_bottom]]):
+    for shift, piece in ((0, own), (1, following), (3, previous), (2, None)):
         columns = pl.ds(pl.multiple_of(lax.rem(group + shift, 4) * width, TILE), width)
-        for source, target in zip(pair, targets):
-            target[:, columns] = source[...]
-
-
-def power_gram(group, pieces, factor, basis, power, mat):
-    order, width = pieces[3].shape
-    collect(group, pieces, (factor, basis))
+        for part, targets in enumerate((tops, bottoms)):
+            source = (far_top, far_bottom)[part] if piece is None else piece
+            start = 0 if piece is None else part * half
+            for target in targets:
+                rows = target.shape[0]
+                target[:, columns] = source[start : start + rows, :]
+                start += rows
+
+
+def power_gram(width, factor, basis, power, mat):
+    order = mat.shape[0]
     for c in range(0, order, width):
         power[:, c : c + width] = dot(factor[...], basis[:, c : c + width]).astype(BF16)
     for c in range(0, order, width):
@@ -193,20 +196,22 @@
 
 def left_kernel(first, *refs):
     pieces, (fresh, mixer, factor, basis, power, mat), work = refs[:5], refs[5:11], refs[11:]
-    power_gram(first[0], pieces, factor, basis, power, mat)
+    collect(first[0], pieces, (factor,), (basis,))
+    power_gram(pieces[3].shape[1], factor, basis, power, mat)
     invert(mat, *work)
     fresh[...] = fresh_of(power, mat[...])
     mixer[...] = dot(fresh[...], basis[...], ((0,), (0,))).astype(BF16)
 
 
 def right_kernel(first, *refs):
-    pieces, moment_pieces, mixer = refs[:5], refs[5:10], refs[10]
-    (fresh, out, factor, basis, power, mat, moment), work = refs[11:18], refs[18:]
+    pieces, mixer = refs[:5], refs[5]
+    (fresh, out, factor, basis, power, mat, moment), work = refs[6:13], refs[13:]
     group = first[0]
     half = moment.shape[0] // 2
     width = fresh.shape[1]
-    power_gram(group, pieces, factor, basis, power, mat)
-    collect(group, moment_pieces, [moment.at[pl.ds(half * t, half), :] for t in range(2)])
+    upper, lower = (moment.at[pl.ds(half * t, half), :] for t in range(2))
+    collect(group, pieces, (factor, upper), (basis, lower))
+    power_gram(width, factor, basis, power, mat)
     carried = dot(moment[...], basis[...], ((1,), (1,))).astype(BF16)
     moment[...] = carried
     invert(mat, *work)
@@ -219,7 +224,7 @@
 SMEM = pl.BlockSpec(memory_space=pltpu.SMEM)
 
 
-def basis_call(kernel, group_index, inputs, order, out_shapes, extra, name):
+def basis_call(kernel, group_index, inputs, order, out_shapes, extra, vmem, name):
     square = pltpu.VMEM((order, order), BF16)
     return pl.pallas_call(
         kernel,
@@ -233,7 +238,7 @@
             pltpu.VMEM((TILE, order), F32),
             pltpu.VMEM((order, TILE), F32),
         ],
-        compiler_params=pltpu.CompilerParams(vmem_limit_bytes=40 * 2**20),
+        compiler_params=pltpu.CompilerParams(vmem_limit_bytes=vmem * 2**20),
         cost_estimate=pl.CostEstimate(
             flops=5 * 10**7 * order, bytes_accessed=10 * order**2, transcendentals=0
         ),
@@ -244,19 +249,21 @@
 def left_call(group_index, pieces):
     order = pieces[3].shape[0]
     shapes = [(order, order)] * 2
-    return basis_call(left_kernel, group_index, pieces, order, shapes, [], "left_basis")
-
-
-def right_call(group_index, pieces, moment_pieces, mixer):
+    return basis_call(left_kernel, group_index, pieces, order, shapes, [], 40, "left_basis")
+
+
+def right_call(group_index, pieces, mixer):
+    rows = mixer.shape[0]
     order, width = pieces[3].shape
-    rows = mixer.shape[0]
+    order -= rows // 2
     return basis_call(
         right_kernel,
         group_index,
-        (*pieces, *moment_pieces, mixer),
+        (*pieces, mixer),
         order,
         [(order, width), (rows, width)],
         [pltpu.VMEM((rows, order), BF16)],
+        56,
         "right_basis",
     )
 
@@ -302,7 +309,7 @@
         ),
         in_specs=[SMEM] * 4 + [VMEM] * 5,
         out_specs=VMEM,
-        compiler_params=pltpu.CompilerParams(vmem_limit_bytes=24 * 2**20),
+        compiler_params=pltpu.CompilerParams(vmem_limit_bytes=56 * 2**20),
         cost_estimate=pl.CostEstimate(flops=10**9, bytes_accessed=4 * 2**20, transcendentals=0),
         name="packed",
     )(places, blocks, row_extent, col_extent, *arrays)
@@ -320,17 +327,6 @@
 def gathered(piece, previous, following):
     half = piece.shape[0] // 2
     return piece, following, previous, shifted(previous[:half], 1), shifted(following[half:], -1)
-
-
-def gathered_at_once(piece):
-    half = piece.shape[0] // 2
-    return (
-        piece,
-        shifted(piece, -1),
-        shifted(piece, 1),
-        shifted(piece[:half], 2),
-        shifted(piece[half:], -2),
-    )
 
 
 def eye_piece(row_count, col_count, col_start):
@@ -402,7 +398,8 @@
         pack[:, start:stop].reshape(-1, right_cols) for start, stop in zip(bounds, bounds[1:])
     )
     left_piece = jnp.concatenate([left_pair[:, :left_cols], left_pair[:, left_cols:]], axis=0)
-    right_piece = jnp.concatenate([factor_r, basis_r], axis=0)
+    half = order_l // 2
+    right_piece = jnp.concatenate([factor_r, moment_in[:half], basis_r, moment_in[half:]], axis=0)
 
     left_pieces = gathered(left_piece, *near(left_piece))
     left_pieces, right_piece = lax.optimization_barrier((left_pieces, right_piece))
@@ -411,10 +408,8 @@
     fresh_l, right_near = lax.optimization_barrier((fresh_l, right_near))
     left_new = lax.dynamic_slice_in_dim(fresh_l, group_index * left_cols, left_cols, 1)
     rows_l = swap(left_new.reshape(owner_count, left_rows, left_cols))
-    right_near, moment_in = lax.optimization_barrier((right_near, moment_in))
     right_pieces = gathered(right_piece, *right_near)
-    moment_pieces = gathered_at_once(moment_in)
-    fresh_r, moment_out = right_call(group, right_pieces, moment_pieces, mixer)
+    fresh_r, moment_out = right_call(group, right_pieces, mixer)
     fresh_r, rows_l = lax.optimization_barrier((fresh_r, rows_l))
 
     by_row = fresh_r.reshape(owner_count, MOST, left_rows, right_cols)
@@ -438,12 +433,14 @@
     def slots(own, second):
         order, width = own.shape
         unit = eye_piece(order, width, group_index * width)
-        filled = (
-            lax.dynamic_index_in_dim(has, fsdp_index, keepdims=False)
-            for has in (has_first, has_second)
+        filled = jnp.stack(
+            [
+                lax.dynamic_index_in_dim(has, fsdp_index, keepdims=False)
+                for has in (has_first, has_second)
+            ]
         )
-        pair = [jnp.where(has, new.astype(F32), unit) for has, new in zip(filled, (own, second))]
-        return jnp.stack(pair)[None]
+        pair = jnp.stack([own, second]).astype(F32)
+        return jnp.where(filled[:, None, None], pair, unit)[None]
 
     return (slots(fresh_r, second_r), slots(left_new, second_l), new_moment)
 

time: 252 us -> 236 us (0.937)
  local copies, waits for them, and re-layouts: 19.2 us -> 9.16 us
  starting transfers between devices: 47.2 us -> 38 us
  Pallas kernels: 65.2 us -> 69.4 us
    unnamed x28 -> x14, local copies, waits for them, and re-layouts: 10.3 us -> 2.56 us
    all_to_all x3, starting transfers between devices: 32.1 us -> 27.5 us  [swap(): lax.all_to_all(pieces, 'fsdp', split_axis=0, concat_axis=0, tiled=True)]
    ppermute x12 -> x8, starting transfers between devices: 15 us -> 10.6 us  [shifted(): lax.ppermute(piece, 'grp', [(i, (i + shift) % count) for i in range(count)])]
    ppermute x12 -> x8, waiting for transfers between devices: 19.6 us -> 16.5 us  [shifted(): lax.ppermute(piece, 'grp', [(i, (i + shift) % count) for i in range(count)])]
  transfers between devices with their start and end apart: 15 -> 11, of which waited for: 7 -> 7; matrix products, arithmetic and copies ran while one was open for 3% -> 3% of each run, Pallas kernels for 25% -> 28%
where the time goes in v1:
time: 236 us; the launch traced here: 235 us
  Pallas kernels  69.4 us (29%)
  waiting for transfers between devices  54.5 us (23%)
  blocking collectives  52.8 us (22%)
  starting transfers between devices  38 us (16%)
  other arithmetic  10.2 us (4%)
  local copies, waits for them, and re-layouts  9.16 us (4%)
    pallas_call x2, Pallas kernels, basis_call(): pl.pallas_call(kernel, out_shape=tuple((jax.ShapeDtypeStruct(shape, BF16)...  65.8 us
    all_to_all x1, blocking collectives, swap(): lax.all_to_all(pieces, 'fsdp', split_axis=0, concat_axis=0, tiled=True)  52.8 us
    all_to_all x3, waiting for transfers between devices, swap(): lax.all_to_all(pieces, 'fsdp', split_axis=0, concat_axis=0, tiled=True)  38 us
    all_to_all x3, starting transfers between devices, swap(): lax.all_to_all(pieces, 'fsdp', split_axis=0, concat_axis=0, tiled=True)  27.5 us
    ppermute x8, waiting for transfers between devices, shifted(): lax.ppermute(piece, 'grp', [(i, (i + shift) % count) for i in range(count)])  16.5 us
    ppermute x8, starting transfers between devices, shifted(): lax.ppermute(piece, 'grp', [(i, (i + shift) % count) for i in range(count)])  10.6 us
  transfers between devices with their start and end apart: 11, of which 7 were waited for; matrix products, arithmetic and copies ran while one was open for 3% of the time, Pallas kernels for 28%

profile of v1, /device:TPU:1, one launch (start us, length us, event | category | flops | bytes accessed | tf_op | source)
XLA Modules:
  0.0 235.0 jit_solution(5713411778481607032)
XLA Ops:
  0.6 0.9 fusion.9
  1.6 0.8 fusion.7
  2.3 0.8 select_reduce_fusion.3
  3.2 0.1 select_reduce_fusion.5
  3.3 0.2 select_reduce_fusion.1
  3.5 0.6 add.28.blocks
  4.1 0.6 pad_add_fusion.1.places
  4.7 3.6 %packed.1 = bf16[64,48,256]{2,1,0:T(8,128)(2,1)} custom-call(s32[2]{0:T(128)} %pad_add_fusion.1.places, s32[64]{0:T(128)} %add.28.blocks, s32[64]{0:T(128)} %row_extent.1, s32[64]{0:T(128)} %col_extent.1, bf16[64,16,256]{2,1,0:T(8,128)(2,1)} %factor_r.1, bf16[64,8,128]{2,1,0:T(8,128)(2,1)} %factor_l.1, f32[64,16,256]{2,1,0:T(8,128)} %basis_r.1, ...), custom_call_target="tpu_custom_call" | custom-call | flops 1000000000 | bytes 4194304 | tf_op jit(solution)/shard_map/packed/pallas_call | solution.py:305
  8.2 52.8 %all_to_all.20 = bf16[64,48,256]{2,1,0:T(8,128)(2,1)S(1)} all-to-all(bf16[64,48,256]{2,1,0:T(8,128)(2,1)} %packed.1), channel_id=1, replica_groups=mesh['fsdp'=64,'grp'=4] {'fsdp'}, dimensions={0} | all-to-all | bytes 3145728 | tf_op jit(solution)/shard_map/all_to_all | solution.py:368
  61.1 1.4 collective-permute-start.1
  62.5 1.5 collective-permute-start
  64.0 0.1 fusion.10
  64.1 6.2 %collective-permute-done.1.refs_2_ = bf16[1024,128]{1,0:T(8,128)(2,1)S(1)} collective-permute-done((bf16[1024,128]{1,0:T(8,128)(2,1)S(1)}, bf16[1024,128]{1,0:T(8,128)(2,1)S(1)}, u32[]{:S(2)}, u32[]{:S(2)}) %collective-permute-start.1) | collective-permute-done | bytes 262176 | tf_op jit(solution)/shard_map/ppermute | solution.py:320
  70.3 0.1 collective-permute-start.2
  70.4 0.0 collective-permute-done.refs_1_
  70.4 2.7 %collective-permute-start.3 = (bf16[512,128]{1,0:T(8,128)(2,1)S(1)}, bf16[512,128]{1,0:T(8,128)(2,1)S(1)}, u32[]{:S(2)}, u32[]{:S(2)}) collective-permute-start(bf16[512,128]{1,0:T(8,128)(2,1)S(1)} %slice.93), channel_id=1, source_target_pairs={{0,3},{1,0},{2,1},{3,2},{4,7},{5,4},{6,5},{7,6},{8,11},{9,8},{10,9... | collective-permute-start | bytes 393224 | tf_op jit(solution)/shard_map/ppermute | solution.py:320
  73.1 0.1 pad_maximum_fusion.refs_0_
  73.2 0.0 copy-start.2
  73.2 2.5 %collective-permute-done.2.refs_3_ = bf16[512,128]{1,0:T(8,128)(2,1)S(1)} collective-permute-done((bf16[512,128]{1,0:T(8,128)(2,1)S(1)}, bf16[512,128]{1,0:T(8,128)(2,1)S(1)}, u32[]{:S(2)}, u32[]{:S(2)}) %collective-permute-start.2) | collective-permute-done | bytes 131104 | tf_op jit(solution)/shard_map/ppermute | solution.py:320
  75.7 0.0 collective-permute-done.3.refs_4_
  75.7 0.1 collective-permute-start.4
  75.8 2.6 %collective-permute-start.5 = (bf16[2560,256]{1,0:T(8,128)(2,1)S(1)}, bf16[2560,256]{1,0:T(8,128)(2,1)S(1)}, u32[]{:S(2)}, u32[]{:S(2)}) collective-permute-start(bf16[2560,256]{1,0:T(8,128)(2,1)S(1)} %pad_maximum_fusion.refs_0_), channel_id=1, source_target_pairs={{0,3},{1,0},{2,1},{3,2},{4,7},{5,4},{6,5},{7,6},{8,11},{9,8},{10,9... | collective-permute-start | bytes 3932168 | tf_op jit(solution)/shard_map/ppermute | solution.py:320
  78.4 19.3 %left_basis.1 = (bf16[512,512]{1,0:T(8,128)(2,1)S(1)}, bf16[512,512]{1,0:T(8,128)(2,1)S(1)}) custom-call(s32[1]{0:T(128)} %bitcast.first, bf16[1024,128]{1,0:T(8,128)(2,1)S(1)} %pad_maximum_fusion.3.refs_0_, bf16[1024,128]{1,0:T(8,128)(2,1)S(1)} %collective-permute-done.refs_1_, bf16[1024,128]{1,0:T(8,128)(2,1)S(1)} %collective-permute-done.1.refs_2_, ...), custom_call_target="tpu_custom_call" | custom-call | flops 25600000000 | bytes 2621440 | tf_op jit(solution)/shard_map/left_basis/pallas_call | solution.py:229
  97.7 0.0 copy-done.2
  97.7 0.0 copy-start
  97.7 0.8 copy-done
  98.5 6.9 %collective-permute-done.4.refs_2_ = bf16[2560,256]{1,0:T(8,128)(2,1)S(1)} collective-permute-done((bf16[2560,256]{1,0:T(8,128)(2,1)S(1)}, bf16[2560,256]{1,0:T(8,128)(2,1)S(1)}, u32[]{:S(2)}, u32[]{:S(2)}) %collective-permute-start.4) | collective-permute-done | bytes 1310752 | tf_op jit(solution)/shard_map/ppermute | solution.py:320
  105.4 0.0 copy-start.3
  105.4 0.0 collective-permute-done.5.refs_1_
  105.4 0.0 copy-start.4
  105.4 0.2 collective-permute-start.6
  105.7 0.8 copy-done.3
  106.5 0.4 copy-done.4
  106.9 2.0 collective-permute-start.7
  108.8 0.7 dynamic-slice_bitcast_fusion
  109.5 10.0 %all-to-all-start.1 = ((bf16[64,8,128]{2,1,0:T(8,128)(2,1)}), bf16[64,8,128]{2,1,0:T(8,128)(2,1)S(1)}, u32[]{:S(2)}, u32[]{:S(2)}) async-start(bf16[64,8,128]{2,1,0:T(8,128)(2,1)} %get-tuple-element.44), calls=%async_computation.1 | async-start | bytes 262144 | tf_op jit(solution)/shard_map/all_to_all | solution.py:368
  119.5 0.7 collective-permute-done.6.refs_3_
  120.2 0.0 copy-start.6
  120.2 0.3 collective-permute-done.7.refs_4_
  120.5 0.6 copy-done.6
  121.0 46.5 %right_basis.1 = (bf16[1024,256]{1,0:T(8,128)(2,1)}, bf16[512,256]{1,0:T(8,128)(2,1)}) custom-call(s32[1]{0:T(128)} %bitcast.first, bf16[2560,256]{1,0:T(8,128)(2,1)} %copy-done.2, bf16[2560,256]{1,0:T(8,128)(2,1)} %copy-done.4, bf16[2560,256]{1,0:T(8,128)(2,1)} %copy-done.3, bf16[1280,256]{1,0:T(8,128)(2,1)} %copy-done.6, ...), custom_call_target="tpu_custom_call" | custom-call | flops 51200000000 | bytes 10485760 | tf_op jit(solution)/shard_map/right_basis/pallas_call | solution.py:229
  167.6 0.0 all-to-all-done.1
  167.6 1.1 slice_bitcast_fusion.3
  168.7 0.6 gather_fusion
  169.3 0.0 copy-start.5
  169.3 1.9 pad_maximum_fusion.1
  171.2 11.2 %all-to-all-start.2 = ((bf16[64,8,896]{2,1,0:T(8,128)(2,1)}), bf16[64,8,896]{2,1,0:T(8,128)(2,1)S(1)}, u32[]{:S(2)}, u32[]{:S(2)}) async-start(bf16[64,8,896]{2,1,0:T(8,128)(2,1)} %pad_maximum_fusion.1), calls=%async_computation.2 | async-start | bytes 1835008 | tf_op jit(solution)/shard_map/all_to_all | solution.py:368
  182.5 0.6 dynamic_slice.13
  183.1 0.6 dynamic_slice.12
  183.7 0.0 copy-done.5
  183.7 0.1 select_reduce_fusion
  183.8 24.4 %all-to-all-done.2 = bf16[64,8,896]{2,1,0:T(8,128)(2,1)S(1)} async-done(((bf16[64,8,896]{2,1,0:T(8,128)(2,1)}), bf16[64,8,896]{2,1,0:T(8,128)(2,1)S(1)}, u32[]{:S(2)}, u32[]{:S(2)}) %all-to-all-start.2) | async-done | bytes 917536 | tf_op jit(solution)/shard_map/all_to_all | solution.py:368
  208.3 1.4 gather_fusion.1
  209.7 6.2 %all-to-all-start.3 = ((bf16[64,8,512]{2,1,0:T(8,128)(2,1)}), bf16[64,8,512]{2,1,0:T(8,128)(2,1)S(1)}, u32[]{:S(2)}, u32[]{:S(2)}) async-start(bf16[64,8,512]{2,1,0:T(8,128)(2,1)} %gather_fusion.1), calls=%async_computation.3 | async-start | bytes 1048576 | tf_op jit(solution)/shard_map/all_to_all | solution.py:368
  215.9 1.4 pad_add_fusion
  217.3 0.1 fusion
  217.4 1.3 gather_fusion.2
  218.7 0.9 convert_select_fusion.1
  219.6 0.0 copy-start.1
  219.6 13.6 %all-to-all-done.3 = bf16[64,8,512]{2,1,0:T(8,128)(2,1)S(1)} async-done(((bf16[64,8,512]{2,1,0:T(8,128)(2,1)}), bf16[64,8,512]{2,1,0:T(8,128)(2,1)S(1)}, u32[]{:S(2)}, u32[]{:S(2)}) %all-to-all-start.3) | async-done | bytes 524320 | tf_op jit(solution)/shard_map/all_to_all | solution.py:368
  233.3 0.1 pad_maximum_fusion.2
  233.4 0.0 copy-done.1
  233.4 1.6 convert_select_fusion
  (20 shorter events, 0.4 us)
Async XLA Ops:
  61.1 9.2 %collective-permute-start.1 = (bf16[1024,128]{1,0:T(8,128)(2,1)S(1)}, bf16[1024,128]{1,0:T(8,128)(2,1)S(1)}, u32[]{:S(2)}, u32[]{:S(2)}) collective-permute-start(bf16[1024,128]{1,0:T(8,128)(2,1)S(1)} %pad_maximum_fusion.3.refs_0_), channel_id=1, source_target_pairs={{0,1},{1,2},{2,3},{3,0},{4,5},{5,6},{6,7},{7,4},{8,9},{9,10},{10,1... | collective-permute-start | bytes 786440 | tf_op jit(solution)/shard_map/ppermute | solution.py:320
  62.5 7.9 %collective-permute-start = (bf16[1024,128]{1,0:T(8,128)(2,1)S(1)}, bf16[1024,128]{1,0:T(8,128)(2,1)S(1)}, u32[]{:S(2)}, u32[]{:S(2)}) collective-permute-start(bf16[1024,128]{1,0:T(8,128)(2,1)S(1)} %pad_maximum_fusion.3.refs_0_), channel_id=1, source_target_pairs={{0,3},{1,0},{2,1},{3,2},{4,7},{5,4},{6,5},{7,6},{8,11},{9,8},{10,9... | collective-permute-start | bytes 786440 | tf_op jit(solution)/shard_map/ppermute | solution.py:320
  70.3 5.4 %collective-permute-start.2 = (bf16[512,128]{1,0:T(8,128)(2,1)S(1)}, bf16[512,128]{1,0:T(8,128)(2,1)S(1)}, u32[]{:S(2)}, u32[]{:S(2)}) collective-permute-start(bf16[512,128]{1,0:T(8,128)(2,1)S(1)} %slice.92), channel_id=1, source_target_pairs={{0,1},{1,2},{2,3},{3,0},{4,5},{5,6},{6,7},{7,4},{8,9},{9,10},{10,1... | collective-permute-start | bytes 393224 | tf_op jit(solution)/shard_map/ppermute | solution.py:320
  70.4 5.3 %collective-permute-start.3 = (bf16[512,128]{1,0:T(8,128)(2,1)S(1)}, bf16[512,128]{1,0:T(8,128)(2,1)S(1)}, u32[]{:S(2)}, u32[]{:S(2)}) collective-permute-start(bf16[512,128]{1,0:T(8,128)(2,1)S(1)} %slice.93), channel_id=1, source_target_pairs={{0,3},{1,0},{2,1},{3,2},{4,7},{5,4},{6,5},{7,6},{8,11},{9,8},{10,9... | collective-permute-start | bytes 393224 | tf_op jit(solution)/shard_map/ppermute | solution.py:320
  73.2 24.4 %copy-start.2 = (bf16[2560,256]{1,0:T(8,128)(2,1)}, bf16[2560,256]{1,0:T(8,128)(2,1)S(1)}, u32[]{:S(2)}) copy-start(bf16[2560,256]{1,0:T(8,128)(2,1)S(1)} %pad_maximum_fusion.refs_0_) | copy-start | bytes 3932164
  75.7 29.7 %collective-permute-start.4 = (bf16[2560,256]{1,0:T(8,128)(2,1)S(1)}, bf16[2560,256]{1,0:T(8,128)(2,1)S(1)}, u32[]{:S(2)}, u32[]{:S(2)}) collective-permute-start(bf16[2560,256]{1,0:T(8,128)(2,1)S(1)} %pad_maximum_fusion.refs_0_), channel_id=1, source_target_pairs={{0,1},{1,2},{2,3},{3,0},{4,5},{5,6},{6,7},{7,4},{8,9},{9,10},{10,1... | collective-permute-start | bytes 3932168 | tf_op jit(solution)/shard_map/ppermute | solution.py:320
  75.8 29.6 %collective-permute-start.5 = (bf16[2560,256]{1,0:T(8,128)(2,1)S(1)}, bf16[2560,256]{1,0:T(8,128)(2,1)S(1)}, u32[]{:S(2)}, u32[]{:S(2)}) collective-permute-start(bf16[2560,256]{1,0:T(8,128)(2,1)S(1)} %pad_maximum_fusion.refs_0_), channel_id=1, source_target_pairs={{0,3},{1,0},{2,1},{3,2},{4,7},{5,4},{6,5},{7,6},{8,11},{9,8},{10,9... | collective-permute-start | bytes 3932168 | tf_op jit(solution)/shard_map/ppermute | solution.py:320
  97.7 0.8 copy-start
  105.4 1.1 copy-start.3
  105.4 1.5 copy-start.4
  105.4 14.8 %collective-permute-start.6 = (bf16[1280,256]{1,0:T(8,128)(2,1)S(1)}, bf16[1280,256]{1,0:T(8,128)(2,1)S(1)}, u32[]{:S(2)}, u32[]{:S(2)}) collective-permute-start(bf16[1280,256]{1,0:T(8,128)(2,1)S(1)} %slice.74), channel_id=1, source_target_pairs={{0,1},{1,2},{2,3},{3,0},{4,5},{5,6},{6,7},{7,4},{8,9},{9,10},{10,1... | collective-permute-start | bytes 1966088 | tf_op jit(solution)/shard_map/ppermute | solution.py:320
  106.9 13.6 %collective-permute-start.7 = (bf16[1280,256]{1,0:T(8,128)(2,1)S(1)}, bf16[1280,256]{1,0:T(8,128)(2,1)}, u32[]{:S(2)}, u32[]{:S(2)}) collective-permute-start(bf16[1280,256]{1,0:T(8,128)(2,1)S(1)} %slice.75), channel_id=1, source_target_pairs={{0,3},{1,0},{2,1},{3,2},{4,7},{5,4},{6,5},{7,6},{8,11},{9,8},{10,9... | collective-permute-start | bytes 1966088 | tf_op jit(solution)/shard_map/ppermute | solution.py:320
  109.5 58.1 %all-to-all-start.1 = ((bf16[64,8,128]{2,1,0:T(8,128)(2,1)}), bf16[64,8,128]{2,1,0:T(8,128)(2,1)S(1)}, u32[]{:S(2)}, u32[]{:S(2)}) async-start(bf16[64,8,128]{2,1,0:T(8,128)(2,1)} %get-tuple-element.44), calls=%async_computation.1 | async-start | bytes 262144 | tf_op jit(solution)/shard_map/all_to_all | solution.py:368
  120.2 0.8 copy-start.6
  169.3 14.4 %copy-start.5 = (s32[64]{0:T(128)S(1)}, s32[64]{0:T(128)}, u32[]{:S(2)}) copy-start(s32[64]{0:T(128)} %add.28.blocks) | copy-start | bytes 772
  171.2 37.0 %all-to-all-start.2 = ((bf16[64,8,896]{2,1,0:T(8,128)(2,1)}), bf16[64,8,896]{2,1,0:T(8,128)(2,1)S(1)}, u32[]{:S(2)}, u32[]{:S(2)}) async-start(bf16[64,8,896]{2,1,0:T(8,128)(2,1)} %pad_maximum_fusion.1), calls=%async_computation.2 | async-start | bytes 1835008 | tf_op jit(solution)/shard_map/all_to_all | solution.py:368
  209.7 23.5 %all-to-all-start.3 = ((bf16[64,8,512]{2,1,0:T(8,128)(2,1)}), bf16[64,8,512]{2,1,0:T(8,128)(2,1)S(1)}, u32[]{:S(2)}, u32[]{:S(2)}) async-start(bf16[64,8,512]{2,1,0:T(8,128)(2,1)} %gather_fusion.1), calls=%async_computation.3 | async-start | bytes 1048576 | tf_op jit(solution)/shard_map/all_to_all | solution.py:368
  219.6 13.7 %copy-start.1 = (bf16[1024,256]{1,0:T(8,128)(2,1)S(1)}, bf16[1024,256]{1,0:T(8,128)(2,1)}, u32[]{:S(2)}) copy-start(bf16[1024,256]{1,0:T(8,128)(2,1)} %get-tuple-element.30) | copy-start | bytes 1572868

commit v2 on v1

--- a/solution.py
+++ b/solution.py
@@ -401,8 +401,8 @@
     half = order_l // 2
     right_piece = jnp.concatenate([factor_r, moment_in[:half], basis_r, moment_in[half:]], axis=0)
 
-    left_pieces = gathered(left_piece, *near(left_piece))
-    left_pieces, right_piece = lax.optimization_barrier((left_pieces, right_piece))
+    left_near, right_piece = lax.optimization_barrier((near(left_piece), right_piece))
+    left_pieces = gathered(left_piece, *left_near)
     right_near = near(right_piece)
     fresh_l, mixer = left_call(group, left_pieces)
     fresh_l, right_near = lax.optimization_barrier((fresh_l, right_near))

time: 236 us -> 233 us (0.987)
    all_to_all x3, starting transfers between devices: 27.5 us -> 24.1 us  [swap(): lax.all_to_all(pieces, 'fsdp', split_axis=0, concat_axis=0, tiled=True)]
  transfers between devices with their start and end apart: 11 -> 11, of which waited for: 7 -> 6; matrix products, arithmetic and copies ran while one was open for 3% -> 3% of each run, Pallas kernels for 28% -> 28%
where the time goes in v2:
time: 233 us; the launch traced here: 232 us
  Pallas kernels  69.4 us (30%)
  waiting for transfers between devices  54.5 us (23%)
  blocking collectives  52.8 us (23%)
  starting transfers between devices  35.9 us (15%)
  other arithmetic  10.2 us (4%)
  local copies, waits for them, and re-layouts  8.44 us (4%)
    pallas_call x2, Pallas kernels, basis_call(): pl.pallas_call(kernel, out_shape=tuple((jax.ShapeDtypeStruct(shape, BF16)...  65.8 us
    all_to_all x1, blocking collectives, swap(): lax.all_to_all(pieces, 'fsdp', split_axis=0, concat_axis=0, tiled=True)  52.8 us
    all_to_all x3, waiting for transfers between devices, swap(): lax.all_to_all(pieces, 'fsdp', split_axis=0, concat_axis=0, tiled=True)  38 us
    all_to_all x3, starting transfers between devices, swap(): lax.all_to_all(pieces, 'fsdp', split_axis=0, concat_axis=0, tiled=True)  24.1 us
    ppermute x8, waiting for transfers between devices, shifted(): lax.ppermute(piece, 'grp', [(i, (i + shift) % count) for i in range(count)])  16.5 us
    ppermute x8, starting transfers between devices, shifted(): lax.ppermute(piece, 'grp', [(i, (i + shift) % count) for i in range(count)])  11.8 us
  transfers between devices with their start and end apart: 11, of which 6 were waited for; matrix products, arithmetic and copies ran while one was open for 3% of the time, Pallas kernels for 28%

profile of v2, /device:TPU:1, one launch (start us, length us, event | category | flops | bytes accessed | tf_op | source)
XLA Modules:
  0.0 232.1 jit_solution(3981752964605360420)
XLA Ops:
  0.6 0.9 fusion.9
  1.6 0.8 fusion.7
  2.3 0.8 select_reduce_fusion.3
  3.2 0.1 select_reduce_fusion.5
  3.3 0.2 select_reduce_fusion.1
  3.5 0.6 add.28.blocks
  4.1 0.6 pad_add_fusion.1.places
  4.7 3.6 %packed.1 = bf16[64,48,256]{2,1,0:T(8,128)(2,1)} custom-call(s32[2]{0:T(128)} %pad_add_fusion.1.places, s32[64]{0:T(128)} %add.28.blocks, s32[64]{0:T(128)} %row_extent.1, s32[64]{0:T(128)} %col_extent.1, bf16[64,16,256]{2,1,0:T(8,128)(2,1)} %factor_r.1, bf16[64,8,128]{2,1,0:T(8,128)(2,1)} %factor_l.1, f32[64,16,256]{2,1,0:T(8,128)} %basis_r.1, ...), custom_call_target="tpu_custom_call" | custom-call | flops 1000000000 | bytes 4194304 | tf_op jit(solution)/shard_map/packed/pallas_call | solution.py:305
  8.2 52.8 %all_to_all.20 = bf16[64,48,256]{2,1,0:T(8,128)(2,1)S(1)} all-to-all(bf16[64,48,256]{2,1,0:T(8,128)(2,1)} %packed.1), channel_id=1, replica_groups=mesh['fsdp'=64,'grp'=4] {'fsdp'}, dimensions={0} | all-to-all | bytes 3145728 | tf_op jit(solution)/shard_map/all_to_all | solution.py:368
  61.1 1.4 collective-permute-start
  62.5 1.5 collective-permute-start.1
  64.0 0.1 fusion.10
  64.1 0.1 pad_maximum_fusion.refs_0_
  64.2 0.0 copy-start.2
  64.2 6.1 %collective-permute-done.refs_2_ = bf16[1024,128]{1,0:T(8,128)(2,1)S(1)} collective-permute-done((bf16[1024,128]{1,0:T(8,128)(2,1)S(1)}, bf16[1024,128]{1,0:T(8,128)(2,1)S(1)}, u32[]{:S(2)}, u32[]{:S(2)}) %collective-permute-start) | collective-permute-done | bytes 262176 | tf_op jit(solution)/shard_map/ppermute | solution.py:320
  70.3 0.0 collective-permute-done.1.refs_1_
  70.3 1.0 collective-permute-start.2
  71.3 1.8 collective-permute-start.3
  73.1 0.0 collective-permute-start.4
  73.1 2.7 %collective-permute-start.5 = (bf16[2560,256]{1,0:T(8,128)(2,1)S(1)}, bf16[2560,256]{1,0:T(8,128)(2,1)S(1)}, u32[]{:S(2)}, u32[]{:S(2)}) collective-permute-start(bf16[2560,256]{1,0:T(8,128)(2,1)S(1)} %pad_maximum_fusion.refs_0_), channel_id=1, source_target_pairs={{0,3},{1,0},{2,1},{3,2},{4,7},{5,4},{6,5},{7,6},{8,11},{9,8},{10,9... | collective-permute-start | bytes 3932168 | tf_op jit(solution)/shard_map/ppermute | solution.py:320
  75.8 0.0 collective-permute-done.2.refs_3_
  75.8 0.0 collective-permute-done.3.refs_4_
  75.8 19.3 %left_basis.1 = (bf16[512,512]{1,0:T(8,128)(2,1)S(1)}, bf16[512,512]{1,0:T(8,128)(2,1)S(1)}) custom-call(s32[1]{0:T(128)} %bitcast.first, bf16[1024,128]{1,0:T(8,128)(2,1)S(1)} %pad_maximum_fusion.3.refs_0_, bf16[1024,128]{1,0:T(8,128)(2,1)S(1)} %collective-permute-done.1.refs_1_, bf16[1024,128]{1,0:T(8,128)(2,1)S(1)} %collective-permute-done.refs_2_, ...), custom_call_target="tpu_custom_call" | custom-call | flops 25600000000 | bytes 2621440 | tf_op jit(solution)/shard_map/left_basis/pallas_call | solution.py:229
  95.1 0.0 copy-done.2
  95.1 0.0 copy-start
  95.1 0.8 copy-done
  95.9 7.3 %collective-permute-done.4.refs_2_ = bf16[2560,256]{1,0:T(8,128)(2,1)S(1)} collective-permute-done((bf16[2560,256]{1,0:T(8,128)(2,1)S(1)}, bf16[2560,256]{1,0:T(8,128)(2,1)S(1)}, u32[]{:S(2)}, u32[]{:S(2)}) %collective-permute-start.4) | collective-permute-done | bytes 1310752 | tf_op jit(solution)/shard_map/ppermute | solution.py:320
  103.2 0.0 copy-start.3
  103.2 0.4 collective-permute-done.5.refs_1_
  103.7 0.0 copy-start.4
  103.7 0.8 collective-permute-start.6
  104.5 0.0 copy-done.3
  104.5 0.2 copy-done.4
  104.7 2.6 %collective-permute-start.7 = (bf16[1280,256]{1,0:T(8,128)(2,1)S(1)}, bf16[1280,256]{1,0:T(8,128)(2,1)}, u32[]{:S(2)}, u32[]{:S(2)}) collective-permute-start(bf16[1280,256]{1,0:T(8,128)(2,1)S(1)} %slice.75), channel_id=1, source_target_pairs={{0,3},{1,0},{2,1},{3,2},{4,7},{5,4},{6,5},{7,6},{8,11},{9,8},{10,9... | collective-permute-start | bytes 1966088 | tf_op jit(solution)/shard_map/ppermute | solution.py:320
  107.4 0.7 dynamic-slice_bitcast_fusion
  108.0 8.5 %all-to-all-start.1 = ((bf16[64,8,128]{2,1,0:T(8,128)(2,1)}), bf16[64,8,128]{2,1,0:T(8,128)(2,1)S(1)}, u32[]{:S(2)}, u32[]{:S(2)}) async-start(bf16[64,8,128]{2,1,0:T(8,128)(2,1)} %get-tuple-element.38), calls=%async_computation.1 | async-start | bytes 262144 | tf_op jit(solution)/shard_map/all_to_all | solution.py:368
  116.6 2.6 %collective-permute-done.6.refs_3_ = bf16[1280,256]{1,0:T(8,128)(2,1)S(1)} collective-permute-done((bf16[1280,256]{1,0:T(8,128)(2,1)S(1)}, bf16[1280,256]{1,0:T(8,128)(2,1)S(1)}, u32[]{:S(2)}, u32[]{:S(2)}) %collective-permute-start.6) | collective-permute-done | bytes 655392 | tf_op jit(solution)/shard_map/ppermute | solution.py:320
  119.2 0.0 copy-start.6
  119.2 0.0 collective-permute-done.7.refs_4_
  119.2 0.8 copy-done.6
  120.0 46.5 %right_basis.1 = (bf16[1024,256]{1,0:T(8,128)(2,1)}, bf16[512,256]{1,0:T(8,128)(2,1)}) custom-call(s32[1]{0:T(128)} %bitcast.first, bf16[2560,256]{1,0:T(8,128)(2,1)} %copy-done.2, bf16[2560,256]{1,0:T(8,128)(2,1)} %copy-done.4, bf16[2560,256]{1,0:T(8,128)(2,1)} %copy-done.3, bf16[1280,256]{1,0:T(8,128)(2,1)} %copy-done.6, ...), custom_call_target="tpu_custom_call" | custom-call | flops 51200000000 | bytes 10485760 | tf_op jit(solution)/shard_map/right_basis/pallas_call | solution.py:229
  166.6 0.0 all-to-all-done.1
  166.6 1.1 slice_bitcast_fusion.3
  167.6 0.6 gather_fusion
  168.3 0.0 copy-start.5
  168.3 1.9 pad_maximum_fusion.1
  170.2 9.4 %all-to-all-start.2 = ((bf16[64,8,896]{2,1,0:T(8,128)(2,1)}), bf16[64,8,896]{2,1,0:T(8,128)(2,1)S(1)}, u32[]{:S(2)}, u32[]{:S(2)}) async-start(bf16[64,8,896]{2,1,0:T(8,128)(2,1)} %pad_maximum_fusion.1), calls=%async_computation.2 | async-start | bytes 1835008 | tf_op jit(solution)/shard_map/all_to_all | solution.py:368
  179.6 0.6 dynamic_slice.13
  180.2 0.6 dynamic_slice.12
  180.8 0.0 copy-done.5
  180.8 0.1 select_reduce_fusion
  180.9 24.4 %all-to-all-done.2 = bf16[64,8,896]{2,1,0:T(8,128)(2,1)S(1)} async-done(((bf16[64,8,896]{2,1,0:T(8,128)(2,1)}), bf16[64,8,896]{2,1,0:T(8,128)(2,1)S(1)}, u32[]{:S(2)}, u32[]{:S(2)}) %all-to-all-start.2) | async-done | bytes 917536 | tf_op jit(solution)/shard_map/all_to_all | solution.py:368
  205.4 1.4 gather_fusion.1
  206.8 6.2 %all-to-all-start.3 = ((bf16[64,8,512]{2,1,0:T(8,128)(2,1)}), bf16[64,8,512]{2,1,0:T(8,128)(2,1)S(1)}, u32[]{:S(2)}, u32[]{:S(2)}) async-start(bf16[64,8,512]{2,1,0:T(8,128)(2,1)} %gather_fusion.1), calls=%async_computation.3 | async-start | bytes 1048576 | tf_op jit(solution)/shard_map/all_to_all | solution.py:368
  213.0 1.4 pad_add_fusion
  214.4 0.1 fusion
  214.6 1.3 gather_fusion.2
  215.9 0.9 convert_select_fusion.1
  216.8 0.0 copy-start.1
  216.8 13.6 %all-to-all-done.3 = bf16[64,8,512]{2,1,0:T(8,128)(2,1)S(1)} async-done(((bf16[64,8,512]{2,1,0:T(8,128)(2,1)}), bf16[64,8,512]{2,1,0:T(8,128)(2,1)S(1)}, u32[]{:S(2)}, u32[]{:S(2)}) %all-to-all-start.3) | async-done | bytes 524320 | tf_op jit(solution)/shard_map/all_to_all | solution.py:368
  230.4 0.1 pad_maximum_fusion.2
  230.5 0.0 copy-done.1
  230.5 1.6 convert_select_fusion
  (20 shorter events, 0.4 us)
Async XLA Ops:
  61.1 9.2 %collective-permute-start = (bf16[1024,128]{1,0:T(8,128)(2,1)S(1)}, bf16[1024,128]{1,0:T(8,128)(2,1)S(1)}, u32[]{:S(2)}, u32[]{:S(2)}) collective-permute-start(bf16[1024,128]{1,0:T(8,128)(2,1)S(1)} %pad_maximum_fusion.3.refs_0_), channel_id=1, source_target_pairs={{0,1},{1,2},{2,3},{3,0},{4,5},{5,6},{6,7},{7,4},{8,9},{9,10},{10,1... | collective-permute-start | bytes 786440 | tf_op jit(solution)/shard_map/ppermute | solution.py:320
  62.5 7.8 %collective-permute-start.1 = (bf16[1024,128]{1,0:T(8,128)(2,1)S(1)}, bf16[1024,128]{1,0:T(8,128)(2,1)S(1)}, u32[]{:S(2)}, u32[]{:S(2)}) collective-permute-start(bf16[1024,128]{1,0:T(8,128)(2,1)S(1)} %pad_maximum_fusion.3.refs_0_), channel_id=1, source_target_pairs={{0,3},{1,0},{2,1},{3,2},{4,7},{5,4},{6,5},{7,6},{8,11},{9,8},{10,9... | collective-permute-start | bytes 786440 | tf_op jit(solution)/shard_map/ppermute | solution.py:320
  64.2 30.9 %copy-start.2 = (bf16[2560,256]{1,0:T(8,128)(2,1)}, bf16[2560,256]{1,0:T(8,128)(2,1)S(1)}, u32[]{:S(2)}) copy-start(bf16[2560,256]{1,0:T(8,128)(2,1)S(1)} %pad_maximum_fusion.refs_0_) | copy-start | bytes 3932164
  70.3 5.5 %collective-permute-start.2 = (bf16[512,128]{1,0:T(8,128)(2,1)S(1)}, bf16[512,128]{1,0:T(8,128)(2,1)S(1)}, u32[]{:S(2)}, u32[]{:S(2)}) collective-permute-start(bf16[512,128]{1,0:T(8,128)(2,1)S(1)} %slice.72), channel_id=1, source_target_pairs={{0,1},{1,2},{2,3},{3,0},{4,5},{5,6},{6,7},{7,4},{8,9},{9,10},{10,1... | collective-permute-start | bytes 393224 | tf_op jit(solution)/shard_map/ppermute | solution.py:320
  71.3 4.5 %collective-permute-start.3 = (bf16[512,128]{1,0:T(8,128)(2,1)S(1)}, bf16[512,128]{1,0:T(8,128)(2,1)S(1)}, u32[]{:S(2)}, u32[]{:S(2)}) collective-permute-start(bf16[512,128]{1,0:T(8,128)(2,1)S(1)} %slice.73), channel_id=1, source_target_pairs={{0,3},{1,0},{2,1},{3,2},{4,7},{5,4},{6,5},{7,6},{8,11},{9,8},{10,9... | collective-permute-start | bytes 393224 | tf_op jit(solution)/shard_map/ppermute | solution.py:320
  73.1 30.1 %collective-permute-start.4 = (bf16[2560,256]{1,0:T(8,128)(2,1)S(1)}, bf16[2560,256]{1,0:T(8,128)(2,1)S(1)}, u32[]{:S(2)}, u32[]{:S(2)}) collective-permute-start(bf16[2560,256]{1,0:T(8,128)(2,1)S(1)} %pad_maximum_fusion.refs_0_), channel_id=1, source_target_pairs={{0,1},{1,2},{2,3},{3,0},{4,5},{5,6},{6,7},{7,4},{8,9},{9,10},{10,1... | collective-permute-start | bytes 3932168 | tf_op jit(solution)/shard_map/ppermute | solution.py:320
  73.1 30.5 %collective-permute-start.5 = (bf16[2560,256]{1,0:T(8,128)(2,1)S(1)}, bf16[2560,256]{1,0:T(8,128)(2,1)S(1)}, u32[]{:S(2)}, u32[]{:S(2)}) collective-permute-start(bf16[2560,256]{1,0:T(8,128)(2,1)S(1)} %pad_maximum_fusion.refs_0_), channel_id=1, source_target_pairs={{0,3},{1,0},{2,1},{3,2},{4,7},{5,4},{6,5},{7,6},{8,11},{9,8},{10,9... | collective-permute-start | bytes 3932168 | tf_op jit(solution)/shard_map/ppermute | solution.py:320
  95.1 0.8 copy-start
  103.2 1.3 copy-start.3
  103.7 1.1 copy-start.4
  103.7 15.5 %collective-permute-start.6 = (bf16[1280,256]{1,0:T(8,128)(2,1)S(1)}, bf16[1280,256]{1,0:T(8,128)(2,1)S(1)}, u32[]{:S(2)}, u32[]{:S(2)}) collective-permute-start(bf16[1280,256]{1,0:T(8,128)(2,1)S(1)} %slice.74), channel_id=1, source_target_pairs={{0,1},{1,2},{2,3},{3,0},{4,5},{5,6},{6,7},{7,4},{8,9},{9,10},{10,1... | collective-permute-start | bytes 1966088 | tf_op jit(solution)/shard_map/ppermute | solution.py:320
  104.7 14.4 %collective-permute-start.7 = (bf16[1280,256]{1,0:T(8,128)(2,1)S(1)}, bf16[1280,256]{1,0:T(8,128)(2,1)}, u32[]{:S(2)}, u32[]{:S(2)}) collective-permute-start(bf16[1280,256]{1,0:T(8,128)(2,1)S(1)} %slice.75), channel_id=1, source_target_pairs={{0,3},{1,0},{2,1},{3,2},{4,7},{5,4},{6,5},{7,6},{8,11},{9,8},{10,9... | collective-permute-start | bytes 1966088 | tf_op jit(solution)/shard_map/ppermute | solution.py:320
  108.0 58.5 %all-to-all-start.1 = ((bf16[64,8,128]{2,1,0:T(8,128)(2,1)}), bf16[64,8,128]{2,1,0:T(8,128)(2,1)S(1)}, u32[]{:S(2)}, u32[]{:S(2)}) async-start(bf16[64,8,128]{2,1,0:T(8,128)(2,1)} %get-tuple-element.38), calls=%async_computation.1 | async-start | bytes 262144 | tf_op jit(solution)/shard_map/all_to_all | solution.py:368
  119.2 0.8 copy-start.6
  168.3 12.6 %copy-start.5 = (s32[64]{0:T(128)S(1)}, s32[64]{0:T(128)}, u32[]{:S(2)}) copy-start(s32[64]{0:T(128)} %add.28.blocks) | copy-start | bytes 772
  170.2 35.2 %all-to-all-start.2 = ((bf16[64,8,896]{2,1,0:T(8,128)(2,1)}), bf16[64,8,896]{2,1,0:T(8,128)(2,1)S(1)}, u32[]{:S(2)}, u32[]{:S(2)}) async-start(bf16[64,8,896]{2,1,0:T(8,128)(2,1)} %pad_maximum_fusion.1), calls=%async_computation.2 | async-start | bytes 1835008 | tf_op jit(solution)/shard_map/all_to_all | solution.py:368
  206.8 23.5 %all-to-all-start.3 = ((bf16[64,8,512]{2,1,0:T(8,128)(2,1)}), bf16[64,8,512]{2,1,0:T(8,128)(2,1)S(1)}, u32[]{:S(2)}, u32[]{:S(2)}) async-start(bf16[64,8,512]{2,1,0:T(8,128)(2,1)} %gather_fusion.1), calls=%async_computation.3 | async-start | bytes 1048576 | tf_op jit(solution)/shard_map/all_to_all | solution.py:368
  216.8 13.7 %copy-start.1 = (bf16[1024,256]{1,0:T(8,128)(2,1)S(1)}, bf16[1024,256]{1,0:T(8,128)(2,1)}, u32[]{:S(2)}) copy-start(bf16[1024,256]{1,0:T(8,128)(2,1)} %get-tuple-element.24) | copy-start | bytes 1572868
